TPU v7x, 32 devices: a whole 2x2x4 slice. The times are simulated.
32 devices in a mesh: expert: 4 (over x, core), shard: 8 (over z, y).
Axes of the slice: x: 2, y: 2, z: 4, core: 2. Of those that a mesh axis runs over, the one named last changes fastest.
Arguments:
- tokens: bfloat16 [65536, 512], P(('expert', 'shard')), may hold values from -6 to 6
- ln1_gain: float32 [512], P(('expert', 'shard')), may hold values from 0.5 to 1.5
- ln2_gain: float32 [512], P(('expert', 'shard')), may hold values from 0.5 to 1.5
- w_query: float32 [512, 512], P(('expert', 'shard')), may hold values from -0.25 to 0.25
- w_key: float32 [512, 512], P(('expert', 'shard')), may hold values from -0.25 to 0.25
- w_value: float32 [512, 512], P(('expert', 'shard')), may hold values from -0.25 to 0.25
- w_attn_out: float32 [512, 512], P(('expert', 'shard')), may hold values from -4 to 4
- w_ctrl: float32 [512, 32], P(('expert', 'shard')), may hold values from -0.1875 to 0.1875
- w_in: float32 [32, 512, 2048], P('expert', None, 'shard'), may hold values from -1 to 1
- b_in: float32 [32, 2048], P('expert', 'shard'), may hold values from -2 to 2
- w_exp_out: float32 [32, 2048, 512], P('expert', 'shard'), may hold values from -1.5 to 1.5
- routes: int32 [2048, 8], P(('expert', 'shard')), may hold values from 0 to 31, all different within a row; in each aligned block of 64 rows (0 to 63, 64 to 127, ...) at most 24 rows name the same one
- grad_out: bfloat16 [65536, 512], P(('expert', 'shard')), may hold values from -6 to 6
Outputs:
- output: bfloat16 [65536, 512], P(('expert', 'shard'))
- grad_tokens: bfloat16 [65536, 512], P(('expert', 'shard'))
- grad_ln1_gain: float32 [512], P(('expert', 'shard'))
- grad_ln2_gain: float32 [512], P(('expert', 'shard'))
- grad_w_query: float32 [512, 512], P(('expert', 'shard'))
- grad_w_key: float32 [512, 512], P(('expert', 'shard'))
- grad_w_value: float32 [512, 512], P(('expert', 'shard'))
- grad_w_attn_out: float32 [512, 512], P(('expert', 'shard'))
- grad_w_ctrl: float32 [512, 32], P(('expert', 'shard'))
- grad_w_in: float32 [32, 512, 2048], P('expert', None, 'shard')
- grad_b_in: float32 [32, 2048], P('expert', 'shard')
- grad_w_exp_out: float32 [32, 2048, 512], P('expert', 'shard')
Inputs may be any that keep to these rules, and one draw needn't show every extreme that they name: `routes`: each row names 8 different experts. Among the rows of one device (aligned blocks of 64 groups) no expert is named more than 24 times, a bound that some block reaches.
All inputs are finite; a program needn't handle non-finite values.
Results may differ from a plain program's by a relative error of at most 0.02.
Values may be sent and summed in bfloat16 or wider, within the bound.
No kernel may reach another device: no remote copies, remote signals or barrier semaphores. Data moves between devices by JAX's collectives and lax.ppermute only.
A program may use at most 256 MiB of HBM per device.

v0:
```python
import jax
import jax.numpy as jnp
from jax import lax
from jax.sharding import PartitionSpec as P

D = 512
HEAD_DIM = 64
HEADS = 8
GROUP = 32
ROUTES = 8
BLOCK = 256
CAP = 24


EPSILON = 1e-05
MASKED = -1e30


def norm_forward(matrix, scale_vec):
    average = jnp.mean(matrix, axis=1, keepdims=True)
    centered = matrix - average
    inverse = lax.rsqrt(jnp.mean(centered * centered, axis=1, keepdims=True) + EPSILON)
    scaled = centered * inverse
    return (scaled * scale_vec, scaled, inverse)


def norm_backward(upstream, scaled, inverse, scale_vec):
    gain_grad = jnp.sum(upstream * scaled, axis=0)
    adjusted = upstream * scale_vec
    first_mean = jnp.mean(adjusted, axis=1, keepdims=True)
    second_mean = jnp.mean(adjusted * scaled, axis=1, keepdims=True)
    return (inverse * (adjusted - first_mean - scaled * second_mean), gain_grad)


def silu_slope(value):
    sigma = jax.nn.sigmoid(value)
    return sigma * (1.0 + value * (1.0 - sigma))


def product(left_op, right_op):
    return jnp.dot(left_op, right_op, preferred_element_type=jnp.float32)


def transposed_product(left_op, right_op):
    return lax.dot_general(
        left_op, right_op, (((0,), (0,)), ((), ())), preferred_element_type=jnp.float32
    )


def against_rows(left_op, right_op):
    return lax.dot_general(
        left_op, right_op, (((1,), (1,)), ((), ())), preferred_element_type=jnp.float32
    )


def block_mask(row_start, row_count, key_count):
    query_block = (row_start + jnp.arange(row_count, dtype=jnp.int32)) // BLOCK
    key_block = jnp.arange(key_count, dtype=jnp.int32) // BLOCK
    return query_block[:, None] >= key_block[None, :]


def head_forward(query_rows, key_rows, value_rows, allowed):
    scores = jnp.where(allowed, against_rows(query_rows, key_rows) * 0.125, MASKED)
    row_top = jnp.max(scores, axis=1, keepdims=True)
    weights = jnp.exp(scores - row_top)
    row_total = jnp.sum(weights, axis=1, keepdims=True)
    shares = (weights / row_total).astype(jnp.bfloat16)
    return (product(shares, value_rows), (row_top + jnp.log(row_total))[:, 0])


def head_backward(query_rows, key_rows, value_rows, upstream, logsum, allowed):
    scores = jnp.where(allowed, against_rows(query_rows, key_rows) * 0.125, MASKED)
    shares = jnp.exp(scores - logsum[:, None])
    value_grad = transposed_product(shares.astype(jnp.bfloat16), upstream)
    share_grad = against_rows(upstream, value_rows)
    score_grad = (
        shares * (share_grad - jnp.sum(shares * share_grad, axis=1, keepdims=True))
    ).astype(jnp.bfloat16)
    query_grad = product(score_grad, key_rows) * 0.125
    key_grad = transposed_product(score_grad, query_rows) * 0.125
    return (query_grad, key_grad, value_grad)


def attention_forward(queries, key_rows, value_rows):
    length = queries.shape[1]
    query_count = min(512, length)
    outputs = []
    logsums = []
    for row_start in range(0, length, query_count):
        row_end = row_start + query_count
        allowed = block_mask(row_start, query_count, row_end)

        def one_head(packed):
            return head_forward(packed[0], packed[1], packed[2], allowed)

        attended, logsum = lax.map(
            one_head,
            (queries[:, row_start:row_end], key_rows[:, :row_end], value_rows[:, :row_end]),
        )
        outputs.append(attended)
        logsums.append(logsum)
    return (jnp.concatenate(outputs, axis=1), jnp.concatenate(logsums, axis=1))


def attention_backward(queries, key_rows, value_rows, upstream, logsums):
    length = queries.shape[1]
    query_count = min(512, length)
    query_parts = []
    key_total = jnp.zeros(key_rows.shape, jnp.float32)
    value_total = jnp.zeros(value_rows.shape, jnp.float32)
    for row_start in range(0, length, query_count):
        row_end = row_start + query_count
        allowed = block_mask(row_start, query_count, row_end)

        def one_head(packed):
            return head_backward(packed[0], packed[1], packed[2], packed[3], packed[4], allowed)

        query_grad, key_grad, value_grad = lax.map(
            one_head,
            (
                queries[:, row_start:row_end],
                key_rows[:, :row_end],
                value_rows[:, :row_end],
                upstream[:, row_start:row_end],
                logsums[:, row_start:row_end],
            ),
        )
        query_parts.append(query_grad)
        key_total = key_total.at[:, :row_end].add(key_grad)
        value_total = value_total.at[:, :row_end].add(value_grad)
    return (jnp.concatenate(query_parts, axis=1), key_total, value_total)


def body(
    tokens,
    ln1_gain,
    ln2_gain,
    w_query,
    w_key,
    w_value,
    w_attn_out,
    w_ctrl,
    w_in,
    b_in,
    w_exp_out,
    routes,
    grad_out,
):
    gain_one, gain_two, query_w, key_w, value_w, attn_out_w, ctrl_w = (
        lax.all_gather(ln1_gain.astype(jnp.bfloat16), ("expert", "shard"), axis=0, tiled=True),
        lax.all_gather(ln2_gain.astype(jnp.bfloat16), ("expert", "shard"), axis=0, tiled=True),
        lax.all_gather(w_query.astype(jnp.bfloat16), ("expert", "shard"), axis=0, tiled=True),
        lax.all_gather(w_key.astype(jnp.bfloat16), ("expert", "shard"), axis=0, tiled=True),
        lax.all_gather(w_value.astype(jnp.bfloat16), ("expert", "shard"), axis=0, tiled=True),
        lax.all_gather(w_attn_out.astype(jnp.bfloat16), ("expert", "shard"), axis=0, tiled=True),
        lax.all_gather(w_ctrl.astype(jnp.bfloat16), ("expert", "shard"), axis=0, tiled=True),
    )
    gain_one = gain_one.astype(jnp.float32)
    gain_two = gain_two.astype(jnp.float32)
    length = tokens.shape[0]

    def split_heads(matrix):
        return matrix.reshape(length, HEADS, HEAD_DIM).transpose(1, 0, 2)

    def merge_heads(stacked):
        return stacked.transpose(1, 0, 2).reshape(length, D)

    inputs = tokens.astype(jnp.float32)
    normed_one, scaled_one, inverse_one = norm_forward(inputs, gain_one)
    normed_low = normed_one.astype(jnp.bfloat16)
    queries = split_heads(product(normed_low, query_w).astype(jnp.bfloat16))
    key_rows = split_heads(product(normed_low, key_w).astype(jnp.bfloat16))
    value_rows = split_heads(product(normed_low, value_w).astype(jnp.bfloat16))
    attended, logsums = attention_forward(queries, key_rows, value_rows)
    attended_low = merge_heads(attended).astype(jnp.bfloat16)
    residual = inputs + product(attended_low, attn_out_w)
    normed_two, scaled_two, inverse_two = norm_forward(residual, gain_two)
    normed_mix = normed_two.astype(jnp.bfloat16)
    logits = product(normed_mix, ctrl_w)
    groups = length // GROUP
    experts = ctrl_w.shape[1]
    mix_probs = jax.nn.softmax(logits.reshape(groups, GROUP, experts), axis=1)
    selector = (routes[:, :, None] == jnp.arange(experts, dtype=jnp.int32)[None, None, :]).astype(
        jnp.float32
    )
    chosen = jnp.sum(mix_probs[:, :, None, :] * selector[:, None, :, :], axis=3)
    chosen_low = chosen.astype(jnp.bfloat16)
    members = normed_mix.reshape(groups, GROUP, D)
    mixed = jnp.einsum(
        "gtk,gtd->gkd", chosen_low, members, preferred_element_type=jnp.float32
    ).astype(jnp.bfloat16)
    owners = lax.axis_size("expert")
    local_count = experts // owners
    expert_ids = routes.reshape(-1)
    onehot = (expert_ids[:, None] == jnp.arange(experts, dtype=jnp.int32)[None, :]).astype(
        jnp.int32
    )
    slot_rank = jnp.sum((jnp.cumsum(onehot, axis=0) - 1) * onehot, axis=1)
    slot_of = (
        expert_ids % local_count * (owners * CAP) + expert_ids // local_count * CAP + slot_rank
    )
    dispatch = (jnp.arange(experts * CAP, dtype=jnp.int32)[:, None] == slot_of[None, :]).astype(
        jnp.bfloat16
    )
    outgoing = (
        product(dispatch, mixed.reshape(-1, D))
        .astype(jnp.bfloat16)
        .reshape(local_count, owners * CAP, D)
    )
    arrived = lax.all_to_all(outgoing, "expert", split_axis=1, concat_axis=1, tiled=True)
    first_w, first_b, second_w = (
        lax.all_gather(w_in.astype(jnp.bfloat16), "shard", axis=2, tiled=True),
        lax.all_gather(b_in.astype(jnp.bfloat16), "shard", axis=1, tiled=True),
        lax.all_gather(w_exp_out.astype(jnp.bfloat16), "shard", axis=1, tiled=True),
    )
    pre_act = (
        jnp.einsum("esd,edf->esf", arrived, first_w, preferred_element_type=jnp.float32)
        + first_b.astype(jnp.float32)[:, None, :]
    )
    active = jax.nn.silu(pre_act).astype(jnp.bfloat16)
    results = jnp.einsum(
        "esf,efd->esd", active, second_w, preferred_element_type=jnp.float32
    ).astype(jnp.bfloat16)
    returned = lax.all_to_all(results, "expert", split_axis=1, concat_axis=1, tiled=True)
    gathered_rows = (
        transposed_product(dispatch, returned.reshape(-1, D))
        .astype(jnp.bfloat16)
        .reshape(groups, ROUTES, D)
    )
    mixture = jnp.einsum(
        "gtk,gkd->gtd", chosen_low, gathered_rows, preferred_element_type=jnp.float32
    ).reshape(length, D)
    output = (residual + mixture).astype(jnp.bfloat16)
    upstream = grad_out.astype(jnp.float32)
    members_up = grad_out.reshape(groups, GROUP, D)
    result_grad = jnp.einsum(
        "gtk,gtd->gkd", chosen_low, members_up, preferred_element_type=jnp.float32
    ).astype(jnp.bfloat16)
    chosen_grad = jnp.einsum(
        "gtd,gkd->gtk", members_up, gathered_rows, preferred_element_type=jnp.float32
    )
    outgoing_grad = (
        product(dispatch, result_grad.reshape(-1, D))
        .astype(jnp.bfloat16)
        .reshape(local_count, owners * CAP, D)
    )
    arrived_grad = lax.all_to_all(outgoing_grad, "expert", split_axis=1, concat_axis=1, tiled=True)
    hidden_grad = jnp.einsum(
        "esd,efd->esf", arrived_grad, second_w, preferred_element_type=jnp.float32
    ).astype(jnp.bfloat16)
    pre_grad = (hidden_grad.astype(jnp.float32) * silu_slope(pre_act)).astype(jnp.bfloat16)
    mixed_grad_rows = jnp.einsum(
        "esf,edf->esd", pre_grad, first_w, preferred_element_type=jnp.float32
    ).astype(jnp.bfloat16)
    second_w_grad = jnp.einsum(
        "esf,esd->efd", active, arrived_grad, preferred_element_type=jnp.float32
    )
    first_w_grad = jnp.einsum("esd,esf->edf", arrived, pre_grad, preferred_element_type=jnp.float32)
    first_b_grad = jnp.sum(pre_grad.astype(jnp.float32), axis=1)
    w_in_grad, b_in_grad, w_exp_out_grad = (
        lax.psum_scatter(
            first_w_grad.astype(jnp.bfloat16), "shard", scatter_dimension=2, tiled=True
        ).astype(jnp.float32),
        lax.psum_scatter(
            first_b_grad.astype(jnp.bfloat16), "shard", scatter_dimension=1, tiled=True
        ).astype(jnp.float32),
        lax.psum_scatter(
            second_w_grad.astype(jnp.bfloat16), "shard", scatter_dimension=1, tiled=True
        ).astype(jnp.float32),
    )
    back_grad = lax.all_to_all(mixed_grad_rows, "expert", split_axis=1, concat_axis=1, tiled=True)
    mixed_grad = (
        transposed_product(dispatch, back_grad.reshape(-1, D))
        .astype(jnp.bfloat16)
        .reshape(groups, ROUTES, D)
    )
    chosen_grad = chosen_grad + jnp.einsum(
        "gtd,gkd->gtk", members, mixed_grad, preferred_element_type=jnp.float32
    )
    normed_grad = jnp.einsum(
        "gtk,gkd->gtd", chosen_low, mixed_grad, preferred_element_type=jnp.float32
    ).reshape(length, D)
    prob_grad = jnp.sum(chosen_grad[:, :, :, None] * selector[:, None, :, :], axis=2)
    logit_grad = (
        (mix_probs * (prob_grad - jnp.sum(mix_probs * prob_grad, axis=1, keepdims=True)))
        .reshape(length, experts)
        .astype(jnp.bfloat16)
    )
    normed_grad = normed_grad + against_rows(logit_grad, ctrl_w)
    ctrl_grad = transposed_product(normed_mix, logit_grad)
    norm_two_grad, gain_two_grad = norm_backward(normed_grad, scaled_two, inverse_two, gain_two)
    residual_grad = upstream + norm_two_grad
    branch_grad = residual_grad.astype(jnp.bfloat16)
    attn_out_grad = transposed_product(attended_low, branch_grad)
    attended_grad = split_heads(against_rows(branch_grad, attn_out_w).astype(jnp.bfloat16))
    query_grad, key_grad, value_grad = attention_backward(
        queries, key_rows, value_rows, attended_grad, logsums
    )
    query_flat = merge_heads(query_grad).astype(jnp.bfloat16)
    key_flat = merge_heads(key_grad).astype(jnp.bfloat16)
    value_flat = merge_heads(value_grad).astype(jnp.bfloat16)
    query_w_grad = transposed_product(normed_low, query_flat)
    key_w_grad = transposed_product(normed_low, key_flat)
    value_w_grad = transposed_product(normed_low, value_flat)
    normed_one_grad = (
        against_rows(query_flat, query_w)
        + against_rows(key_flat, key_w)
        + against_rows(value_flat, value_w)
    )
    norm_one_grad, gain_one_grad = norm_backward(normed_one_grad, scaled_one, inverse_one, gain_one)
    input_grad = (residual_grad + norm_one_grad).astype(jnp.bfloat16)
    ln1_grad, ln2_grad, wq_grad, wk_grad, wv_grad, wo_grad, wc_grad = (
        lax.psum_scatter(gain_one_grad, ("expert", "shard"), scatter_dimension=0, tiled=True),
        lax.psum_scatter(gain_two_grad, ("expert", "shard"), scatter_dimension=0, tiled=True),
        lax.psum_scatter(query_w_grad, ("expert", "shard"), scatter_dimension=0, tiled=True),
        lax.psum_scatter(key_w_grad, ("expert", "shard"), scatter_dimension=0, tiled=True),
        lax.psum_scatter(value_w_grad, ("expert", "shard"), scatter_dimension=0, tiled=True),
        lax.psum_scatter(attn_out_grad, ("expert", "shard"), scatter_dimension=0, tiled=True),
        lax.psum_scatter(ctrl_grad, ("expert", "shard"), scatter_dimension=0, tiled=True),
    )
    return (
        output,
        input_grad,
        ln1_grad,
        ln2_grad,
        wq_grad,
        wk_grad,
        wv_grad,
        wo_grad,
        wc_grad,
        w_in_grad,
        b_in_grad,
        w_exp_out_grad,
    )


def solution(mesh):
    in_specs = (
        P(("expert", "shard"), None),
        P(("expert", "shard")),
        P(("expert", "shard")),
        P(("expert", "shard"), None),
        P(("expert", "shard"), None),
        P(("expert", "shard"), None),
        P(("expert", "shard"), None),
        P(("expert", "shard"), None),
        P("expert", None, "shard"),
        P("expert", "shard"),
        P("expert", "shard", None),
        P(("expert", "shard"), None),
        P(("expert", "shard"), None),
    )
    out_specs = (
        P(("expert", "shard"), None),
        P(("expert", "shard"), None),
        P(("expert", "shard")),
        P(("expert", "shard")),
        P(("expert", "shard"), None),
        P(("expert", "shard"), None),
        P(("expert", "shard"), None),
        P(("expert", "shard"), None),
        P(("expert", "shard"), None),
        P("expert", None, "shard"),
        P("expert", "shard"),
        P("expert", "shard", None),
    )
    return jax.shard_map(body, mesh=mesh, in_specs=in_specs, out_specs=out_specs, check_vma=False)
```

profile of v0, /device:TPU:0, one launch (start us, length us, event | category | flops | bytes accessed | tf_op | source)
XLA Modules:
  0.0 2057.0 jit_solution(8967700291530584736)
XLA Ops:
  7.2 3.8 convert_element_type.234
  11.1 3.8 convert_element_type.238
  16.4 58.6 %all-reduce.7 = (bf16[512]{0:T(512)(128)(2,1)S(1)}, bf16[512]{0:T(512)(128)(2,1)S(1)}) all-reduce(bf16[512]{0:T(512)(128)(2,1)S(1)} %dynamic-update-slice.22, bf16[512]{0:T(512)(128)(2,1)S(1)} %dynamic-update-slice.23), channel_id=1, replica_groups=mesh['expert'=4,'shard'=8] {'expert','shard'}, use_global_device_ids=true, to_apply=%add.2 | all-reduce | flops 1024 | bytes 4096
  76.4 98.5 %all_gather.32 = bf16[512,512]{1,0:T(8,128)(2,1)S(1)} all-gather(bf16[16,512]{1,0:T(8,128)(2,1)S(1)} %convert_element_type.218), channel_id=1, replica_groups=mesh['expert'=4,'shard'=8] {'expert','shard'}, dimensions={0}, use_global_device_ids=true | all-gather | bytes 540672 | tf_op jit(solution)/shard_map/all_gather | solution.py:153
  175.7 2.6 convolution_convert_fusion.5
  178.4 4.8 copy.97
  183.2 3.2 slice.258
  188.7 88.6 %all_gather.33 = bf16[512,512]{1,0:T(8,128)(2,1)S(1)} all-gather(bf16[16,512]{1,0:T(8,128)(2,1)S(1)} %convert_element_type.220), channel_id=1, replica_groups=mesh['expert'=4,'shard'=8] {'expert','shard'}, dimensions={0}, use_global_device_ids=true | all-gather | bytes 540672 | tf_op jit(solution)/shard_map/all_gather | solution.py:154
  280.0 4.8 copy.98
  284.7 3.3 slice.259
  290.3 77.3 %all_gather.31 = bf16[512,512]{1,0:T(8,128)(2,1)S(1)} all-gather(bf16[16,512]{1,0:T(8,128)(2,1)S(1)} %convert_element_type.216), channel_id=1, replica_groups=mesh['expert'=4,'shard'=8] {'expert','shard'}, dimensions={0}, use_global_device_ids=true | all-gather | bytes 540672 | tf_op jit(solution)/shard_map/all_gather | solution.py:152
  370.3 4.7 copy.96
  375.0 4.3 fusion.255
  379.3 34.9 %while.131 = (s32[]{:T(128)}, bf16[8,512,64]{1,2,0:T(8,128)(2,1)}, f32[8,512]{1,0:T(8,128)S(1)}, bf16[8,512,64]{2,1,0:T(8,128)(2,1)}, bf16[8,1024,64]{2,1,0:T(8,...) while((s32[]{:T(128)}, bf16[8,512,64]{1,2,0:T(8,128)(2,1)}, ...), condition=%wide.region_9.10_spmd.clone.clone, body=%wide.region_6.9_spmd.clone.sunk.clone | while | flops 138935808 | bytes 7106657 | solution.py:96
  414.8 22.4 %while.130 = (s32[]{:T(128)}, bf16[8,512,64]{1,2,0:T(8,128)(2,1)S(1)}, f32[8,512]{1,0:T(8,128)S(1)}, bf16[8,512,64]{2,1,0:T(8,128)(2,1)}, bf16[8,512,64]{2,1,0:T...) while((s32[]{:T(128)}, bf16[8,512,64]{1,2,0:T(8,128)(2,1)S(1)}, ...), condition=%wide.region_5.6_spmd.clone.clone, body=%wide.region_2.5_spmd.clone.sunk.clone | while | flops 69467648 | bytes 3696729 | solution.py:96
  437.3 4.0 slice.261
  446.2 73.5 %all_gather.36 = bf16[512,32]{1,0:T(8,128)(2,1)S(1)} all-gather(bf16[16,32]{1,0:T(8,128)(2,1)S(1)} %convert_element_type.228), channel_id=1, replica_groups=mesh['expert'=4,'shard'=8] {'expert','shard'}, dimensions={0}, use_global_device_ids=true | all-gather | bytes 33792 | tf_op jit(solution)/shard_map/all_gather | solution.py:156
  519.7 73.5 %all_gather.34 = bf16[512,512]{1,0:T(8,128)(2,1)} all-gather(bf16[16,512]{1,0:T(8,128)(2,1)S(1)} %convert_element_type.224), channel_id=1, replica_groups=mesh['expert'=4,'shard'=8] {'expert','shard'}, dimensions={0}, use_global_device_ids=true | all-gather | bytes 540672 | tf_op jit(solution)/shard_map/all_gather | solution.py:155
  593.2 34.3 %while.132 = (s32[]{:T(128)}, bf16[8,512,64]{1,2,0:T(8,128)(2,1)S(1)}, f32[8,512]{1,0:T(8,128)S(1)}, bf16[8,512,64]{2,1,0:T(8,128)(2,1)}, bf16[8,1536,64]{2,1,0:...) while((s32[]{:T(128)}, ...), condition=%wide.region_13.14_spmd.clone.clone, body=%wide.region_10.13_spmd.clone.sunk.clone | while | flops 208403968 | bytes 10516577 | solution.py:96
  628.2 39.2 %while.133 = (s32[]{:T(128)}, bf16[8,512,64]{1,2,0:T(8,128)(2,1)S(1)}, f32[8,512]{1,0:T(8,128)S(1)}, bf16[8,512,64]{2,1,0:T(8,128)(2,1)}, bf16[8,2048,64]{2,1,0:...) while((s32[]{:T(128)}, ...), condition=%wide.region_17.18_spmd.clone.clone, body=%wide.region_14.17_spmd.clone.sunk.clone | while | flops 277872128 | bytes 13926497 | solution.py:96
  682.3 7.5 all-to-all-start
  689.8 30.9 %all_gather.38 = bf16[8,2048]{1,0:T(8,128)(2,1)S(1)} all-gather(bf16[8,256]{1,0:T(8,128)(2,1)S(1)} %convert_element_type.235), channel_id=1, replica_groups=mesh['expert'=4,'shard'=8] {'shard'}, dimensions={1}, use_global_device_ids=true | all-gather | bytes 36864 | tf_op jit(solution)/shard_map/all_gather | solution.py:213
  725.5 3.5 all-to-all-start.2
  729.1 11.3 fusion.215
  741.6 11.4 fusion.258
  753.2 9.9 convolution_convert_fusion.1
  768.9 10.5 convolution_convert_fusion.8
  780.7 4.2 all-to-all-start.1
  785.2 10.5 convolution_convert_fusion
  795.7 11.9 convolution_convert_fusion.7
  810.2 3.6 all-to-all-start.3
  817.6 2.8 fusion.260
  820.4 5.1 all-to-all-done.3
  826.4 2.7 fusion.261
  839.3 6.1 multiply_reduce_fusion.4
  845.9 3.3 multiply_add_fusion
  849.2 2.7 convolution_convert_fusion.3
  851.9 4.9 copy.120
  856.8 4.4 fusion.254
  861.2 86.8 %while.136 = (s32[]{:T(128)}, bf16[8,512,64]{1,2,0:T(8,128)(2,1)S(1)}, f32[8,1536,64]{1,2,0:T(8,128)}, f32[8,1536,64]{1,2,0:T(8,128)}, bf16[8,512,64]{2,1,0:T(8,...) while((s32[]{:T(128)}, ...), condition=%wide.region_38.39_spmd.clone.clone, body=%wide.region_36.38_spmd.clone.sunk.clone | while | flops 511311360 | bytes 26238072 | solution.py:118
  948.0 68.4 %while.134 = (s32[]{:T(128)}, bf16[8,512,64]{1,2,0:T(8,128)(2,1)S(1)}, f32[8,512,64]{1,2,0:T(8,128)}, f32[8,512,64]{1,2,0:T(8,128)}, bf16[8,512,64]{2,1,0:T(8,12...) while((s32[]{:T(128)}, ...), condition=%wide.region_32.33_spmd.clone.clone, body=%wide.region_30.32_spmd.clone.sunk.clone | while | flops 170458624 | bytes 9194609 | solution.py:118
  1017.9 82.5 %while.135 = (s32[]{:T(128)}, bf16[8,512,64]{1,2,0:T(8,128)(2,1)}, f32[8,1024,64]{1,2,0:T(8,128)}, f32[8,1024,64]{1,2,0:T(8,128)}, bf16[8,512,64]{2,1,0:T(8,128)...) while((s32[]{:T(128)}, bf16[8,512,64]{1,2,0:T(8,128)(2,1)}, ...), condition=%wide.region_35.36_spmd.clone.clone, body=%wide.region_33.35_spmd.clone.sunk.clone | while | flops 340884992 | bytes 17716344 | solution.py:118
  1100.5 95.8 %while.137 = (s32[]{:T(128)}, bf16[8,512,64]{1,2,0:T(8,128)(2,1)S(1)}, f32[8,2048,64]{1,2,0:T(8,128)}, f32[8,2048,64]{1,2,0:T(8,128)}, bf16[8,512,64]{2,1,0:T(8,...) while((s32[]{:T(128)}, ...), condition=%wide.region_41.42_spmd.clone.clone, body=%wide.region_39.41_spmd.clone.sunk.clone | while | flops 681737728 | bytes 34759800 | solution.py:118
  1198.5 3.9 fusion.264
  1202.4 3.9 scatter-add.25
  1208.9 4.6 add_dynamic-update-slice_fusion.1
  1213.6 4.4 fusion.190
  1218.0 2.9 add_convert_fusion.1
  1224.6 4.3 add_dynamic-update-slice_fusion
  1228.9 4.3 fusion.189
  1233.3 2.9 add_convert_fusion
  1241.4 3.4 fusion.262
  1248.3 3.1 fusion.263
  1252.6 4.8 fusion.186
  1257.4 37.2 %all-reduce.6 = (f32[512]{0:T(512)S(1)}, f32[512]{0:T(512)S(1)}) all-reduce(f32[512]{0:T(512)S(1)} %get-tuple-element.692, f32[512]{0:T(512)S(1)} %copy-done.101), channel_id=2, replica_groups=mesh['expert'=4,'shard'=8] {'expert','shard'}, use_global_device_ids=true, to_apply=%region_45.46.clone | all-reduce | flops 1024 | bytes 8192
  1295.7 5.2 fusion.185
  1300.9 4.0 convert_element_type.263
  1304.9 72.8 %reduce-scatter.23.cloned.1.call-done = bf16[8,256,512]{2,1,0:T(8,128)(2,1)} async-done(((bf16[8,2048,512]{2,1,0:T(8,128)(2,1)}), bf16[8,256,512]{2,1,0:T(8,128)(2,1)}) %reduce-scatter.23.cloned.1.call-update) | async-done | bytes 2097168 | tf_op jit(solution)/shard_map/reduce_scatter | solution.py:267
  1377.7 4.2 convert_element_type.266
  1381.9 131.0 %reduce-scatter.17.cloned.1.call-done = f32[16,32]{1,0:T(8,128)} async-done(((f32[512,32]{1,0:T(8,128)}), f32[16,32]{1,0:T(8,128)}) %reduce-scatter.17.cloned.1.call-update) | async-done | bytes 2064 | tf_op jit(solution)/shard_map/reduce_scatter | solution.py:319
  1512.9 134.2 %reduce-scatter.9.cloned.1.call-done = f32[16,512]{1,0:T(8,128)} async-done(((f32[512,512]{1,0:T(8,128)}), f32[16,512]{1,0:T(8,128)}) %reduce-scatter.9.cloned.1.call-update) | async-done | bytes 32784 | tf_op jit(solution)/shard_map/reduce_scatter | solution.py:315
  1647.1 134.3 %reduce-scatter.11.cloned.1.call-done = f32[16,512]{1,0:T(8,128)} async-done(((f32[512,512]{1,0:T(8,128)}), f32[16,512]{1,0:T(8,128)}) %reduce-scatter.11.cloned.1.call-update) | async-done | bytes 32784 | tf_op jit(solution)/shard_map/reduce_scatter | solution.py:316
  1781.4 134.3 %reduce-scatter.13.cloned.1.call-done = f32[16,512]{1,0:T(8,128)} async-done(((f32[512,512]{1,0:T(8,128)}), f32[16,512]{1,0:T(8,128)}) %reduce-scatter.13.cloned.1.call-update) | async-done | bytes 32784 | tf_op jit(solution)/shard_map/reduce_scatter | solution.py:317
  1915.7 134.2 %reduce-scatter.15.cloned.1.call-done = f32[16,512]{1,0:T(8,128)} async-done(((f32[512,512]{1,0:T(8,128)}), f32[16,512]{1,0:T(8,128)}) %reduce-scatter.15.cloned.1.call-update) | async-done | bytes 32784 | tf_op jit(solution)/shard_map/reduce_scatter | solution.py:318
  (732 shorter events, 549.1 us)
Async XLA Ops:
  7.2 721.9 %all-gather.3.cloned.1.call-start = ((), (), s32[]{:S(2)}) async-start(), calls=%async_computation.12 | async-start | bytes 18874368 | tf_op jit(solution)/shard_map/all_gather | solution.py:212
  11.0 730.6 %all-gather.5.cloned.1.call-start = ((), (), s32[]{:S(2)}) async-start(), calls=%async_computation.13 | async-start | bytes 18874368 | tf_op jit(solution)/shard_map/all_gather | solution.py:214
  14.9 60.1 %copy-start.2 = (bf16[2048,512]{1,0:T(8,128)(2,1)S(1)}, bf16[2048,512]{1,0:T(8,128)(2,1)}, u32[]{:S(2)}) copy-start(bf16[2048,512]{1,0:T(8,128)(2,1)} %param.49) | copy-start | bytes 6291460
  14.9 422.3 %copy-start.6 = (bf16[8,512,64]{1,2,0:T(8,128)(2,1)}, bf16[8,512,64]{1,2,0:T(8,128)(2,1)S(1)}, u32[]{:S(2)}) copy-start(bf16[8,512,64]{1,2,0:T(8,128)(2,1)S(1)} %fusion.256) | copy-start | bytes 1572868
  15.0 61.4 %copy-start.88 = (f32[16,512]{1,0:T(8,128)S(1)}, f32[16,512]{1,0:T(8,128)}, u32[]{:S(2)}) copy-start(f32[16,512]{1,0:T(8,128)} %param.53) | copy-start | bytes 98308
  74.9 99.9 %copy-start.92 = (f32[512]{0:T(512)}, f32[512]{0:T(512)S(1)}, u32[]{:S(2)}) copy-start(f32[512]{0:T(512)S(1)} %convert_element_type.214) | copy-start | bytes 6148
  75.3 99.6 %copy-start.69 = (f32[2048]{0:T(1024)}, f32[2048]{0:T(1024)S(1)}, u32[]{:S(2)}) copy-start(f32[2048]{0:T(1024)S(1)} %broadcast_multiply_fusion.5) | copy-start | bytes 24580
  76.4 102.0 %copy-start.75 = (f32[2048]{0:T(1024)}, f32[2048]{0:T(1024)S(1)}, u32[]{:S(2)}) copy-start(f32[2048]{0:T(1024)S(1)} %add_rsqrt_fusion.1) | copy-start | bytes 24580
  183.1 5.5 copy-start.89
  183.2 94.2 %copy-start.42 = (bf16[2048,512]{1,0:T(8,128)(2,1)S(1)}, bf16[2048,512]{1,0:T(8,128)(2,1)}, u32[]{:S(2)}) copy-start(bf16[2048,512]{1,0:T(8,128)(2,1)} %copy-done.41) | copy-start | bytes 6291460
  284.7 5.6 copy-start.90
  284.7 82.9 %copy-start.43 = (bf16[2048,512]{1,0:T(8,128)(2,1)S(1)}, bf16[2048,512]{1,0:T(8,128)(2,1)}, u32[]{:S(2)}) copy-start(bf16[2048,512]{1,0:T(8,128)(2,1)} %copy-done.41) | copy-start | bytes 6291460
  441.4 4.8 copy-start.102
  441.4 151.8 %copy-start.10 = (bf16[8,512,64]{1,2,0:T(8,128)(2,1)S(1)}, bf16[8,512,64]{1,2,0:T(8,128)(2,1)}, u32[]{:S(2)}) copy-start(bf16[8,512,64]{1,2,0:T(8,128)(2,1)} %copy-done.6) | copy-start | bytes 1572868
  444.2 227.1 %copy-start.94 = (f32[512]{0:T(512)}, f32[512]{0:T(512)S(1)}, u32[]{:S(2)}) copy-start(f32[512]{0:T(512)S(1)} %convert_element_type.226) | copy-start | bytes 6148
  445.4 147.8 %copy-start.56 = (s32[32,4,128]{2,0,1:T(8,128)}, s32[32,4,128]{2,0,1:T(8,128)S(1)}, u32[]{:S(2)}) copy-start(s32[32,4,128]{2,0,1:T(8,128)S(1)} %reduce-window.6) | copy-start | bytes 196612
  519.7 152.4 %copy-start.49 = (bf16[512,32]{1,0:T(8,128)(2,1)}, bf16[512,32]{1,0:T(8,128)(2,1)S(1)}, u32[]{:S(2)}) copy-start(bf16[512,32]{1,0:T(8,128)(2,1)S(1)} %all_gather.36) | copy-start | bytes 98308
  593.2 34.4 %copy-start.9 = (bf16[8,512,64]{1,2,0:T(8,128)(2,1)S(1)}, bf16[8,512,64]{1,2,0:T(8,128)(2,1)}, u32[]{:S(2)}) copy-start(bf16[8,512,64]{1,2,0:T(8,128)(2,1)} %copy-done.6) | copy-start | bytes 1572868
  672.4 7.7 copy-start.15
  678.4 11.4 copy-start.103
  680.1 41.2 %copy-start.96 = (s32[512]{0:T(512)}, s32[512]{0:T(512)S(1)}, u32[]{:S(2)}) copy-start(s32[512]{0:T(512)S(1)} %fusion.237) | copy-start | bytes 6148
  680.9 40.3 %copy-start.18 = (bf16[2048,512]{1,0:T(8,128)(2,1)S(1)}, bf16[2048,512]{1,0:T(8,128)(2,1)}, u32[]{:S(2)}) copy-start(bf16[2048,512]{1,0:T(8,128)(2,1)} %param.61) | copy-start | bytes 6291460
  682.3 43.2 %all-to-all-start = ((bf16[8,96,512]{2,0,1:T(8,128)(2,1)}), bf16[8,96,512]{2,0,1:T(8,128)(2,1)S(1)}, u32[]{:S(2)}, u32[]{:S(2)}) async-start(bf16[8,96,512]{2,0,1:T(8,128)(2,1)} %copy.104), calls=%async_computation | async-start | bytes 1572864 | tf_op jit(solution)/shard_map/all_to_all | solution.py:210
  725.5 14.9 copy-start.25
  725.5 15.2 all-to-all-start.2
  729.0 511.1 %reduce-scatter.21.cloned.1.call-start = ((), (), s32[]{:S(2)}) async-start(), calls=%async_computation.20 | async-start | bytes 36864 | tf_op jit(solution)/shard_map/reduce_scatter | solution.py:264
  753.0 10.2 copy-start.13
  753.0 547.9 %reduce-scatter.19.cloned.1.call-start = ((), (), s32[]{:S(2)}) async-start(), calls=%async_computation.19 | async-start | bytes 18874368 | tf_op jit(solution)/shard_map/reduce_scatter | solution.py:261
  780.7 29.5 %all-to-all-start.1 = ((bf16[8,96,512]{2,0,1:T(8,128)(2,1)}), bf16[8,96,512]{2,0,1:T(8,128)(2,1)}, u32[]{:S(2)}, u32[]{:S(2)}) async-start(bf16[8,96,512]{2,0,1:T(8,128)(2,1)} %copy.106), calls=%async_computation.1 | async-start | bytes 1572864 | tf_op jit(solution)/shard_map/all_to_all | solution.py:224
  785.0 592.7 %reduce-scatter.23.cloned.1.call-start = ((), (), s32[]{:S(2)}) async-start(), calls=%async_computation.21 | async-start | bytes 18874368 | tf_op jit(solution)/shard_map/reduce_scatter | solution.py:267
  785.2 10.5 copy-start.14
  810.2 5.3 copy-start.97
  810.2 6.0 copy-start.19
  810.2 15.3 all-to-all-start.3
  813.8 699.0 %reduce-scatter.17.cloned.1.call-start = ((), (), s32[]{:S(2)}) async-start(), calls=%async_computation.18 | async-start | bytes 270336 | tf_op jit(solution)/shard_map/reduce_scatter | solution.py:319
  817.6 8.1 copy-start.98
  829.1 4.5 copy-start.28
  833.6 5.6 copy-start.50
  834.5 4.7 copy-start.68
  834.5 4.7 copy-start.74
  839.2 6.1 copy-start.57
  839.2 6.1 copy-start.1
  839.2 6.1 copy-start.20
  839.3 6.7 copy-start.21
  839.3 6.7 copy-start.95
  856.8 4.4 copy-start.11
  856.8 4.4 copy-start.60
  856.8 4.4 copy-start.80
  861.2 86.9 %copy-start.8 = (bf16[8,512,64]{1,2,0:T(8,128)(2,1)S(1)}, bf16[8,512,64]{1,2,0:T(8,128)(2,1)}, u32[]{:S(2)}) copy-start(bf16[8,512,64]{1,2,0:T(8,128)(2,1)} %copy-done.6) | copy-start | bytes 1572868
  861.2 86.9 %copy-start.66 = (s32[512]{0:T(512)S(1)}, s32[512]{0:T(512)}, u32[]{:S(2)}) copy-start(s32[512]{0:T(512)} %copy-done.65) | copy-start | bytes 6148
  948.0 68.4 %copy-start.58 = (bf16[2048,32]{0,1:T(8,128)(2,1)S(1)}, bf16[2048,32]{0,1:T(8,128)(2,1)}, u32[]{:S(2)}) copy-start(bf16[2048,32]{0,1:T(8,128)(2,1)} %copy-done.57) | copy-start | bytes 393220
  1017.9 82.6 %copy-start.46 = (bf16[8,512,64]{1,2,0:T(8,128)(2,1)S(1)}, bf16[8,512,64]{1,2,0:T(8,128)(2,1)}, u32[]{:S(2)}) copy-start(bf16[8,512,64]{1,2,0:T(8,128)(2,1)} %copy.243) | copy-start | bytes 1572868
  1017.9 82.6 %copy-start.62 = (s32[2048]{0:T(1024)S(1)}, s32[2048]{0:T(1024)}, u32[]{:S(2)}) copy-start(s32[2048]{0:T(1024)} %copy-done.61) | copy-start | bytes 24580
  1017.9 82.5 %copy-start.82 = (s32[512]{0:T(512)S(1)}, s32[512]{0:T(512)}, u32[]{:S(2)}) copy-start(s32[512]{0:T(512)} %copy-done.81) | copy-start | bytes 6148
  1196.3 450.8 %reduce-scatter.9.cloned.1.call-start = ((), (), s32[]{:S(2)}) async-start(), calls=%async_computation.14 | async-start | bytes 1081344 | tf_op jit(solution)/shard_map/reduce_scatter | solution.py:315
  1208.9 572.5 %reduce-scatter.11.cloned.1.call-start = ((), (), s32[]{:S(2)}) async-start(), calls=%async_computation.15 | async-start | bytes 1081344 | tf_op jit(solution)/shard_map/reduce_scatter | solution.py:316
  1208.9 4.6 copy-start.33
  1213.6 4.4 copy-start.31
  1224.6 691.2 %reduce-scatter.13.cloned.1.call-start = ((), (), s32[]{:S(2)}) async-start(), calls=%async_computation.16 | async-start | bytes 1081344 | tf_op jit(solution)/shard_map/reduce_scatter | solution.py:317
  1239.9 810.0 %reduce-scatter.15.cloned.1.call-start = ((), (), s32[]{:S(2)}) async-start(), calls=%async_computation.17 | async-start | bytes 1081344 | tf_op jit(solution)/shard_map/reduce_scatter | solution.py:318
  1241.4 4.5 copy-start.23
  1248.2 4.4 copy-start.38
  1248.2 4.4 copy-start.70
  1252.6 4.8 copy-start.101
  (56 other events, 147.2 us)
Sparse Core Ops, SparseCore 0:
  11.1 243.9 all-gather.2
  257.3 232.2 all-gather.4
  753.1 52.8 reduce-scatter.20
  809.6 281.6 reduce-scatter.18
  1095.5 282.1 reduce-scatter.22
  1380.3 132.4 reduce-scatter.16
  1515.8 131.2 reduce-scatter.8
  1649.9 131.4 reduce-scatter.10
  1784.3 131.3 reduce-scatter.12
  1918.4 131.4 reduce-scatter.14
where the time goes:
time: 2070 us; the launch traced here: 2060 us
  waiting for transfers between devices  746 us (36%)
  blocking collectives  538 us (26%)
  matrix products  531 us (26%)
  local copies, waits for them, and re-layouts  110 us (5%)
  other arithmetic  93.5 us (5%)
    dot_general x101, matrix products, against_rows(): lax.dot_general(left_op, right_op, (((1,), (1,)), ((), ())), preferred_el...  188 us
    dot_general x71, matrix products, transposed_product(): lax.dot_general(left_op, right_op, (((0,), (0,)), ((), ())), preferred_el...  144 us
    reduce_scatter x1, waiting for transfers between devices, body(): lax.psum_scatter(value_w_grad, ('expert', 'shard'), scatter_dimension=0,...  134 us
    reduce_scatter x1, waiting for transfers between devices, body(): lax.psum_scatter(key_w_grad, ('expert', 'shard'), scatter_dimension=0, ti...  134 us
    reduce_scatter x1, waiting for transfers between devices, body(): lax.psum_scatter(query_w_grad, ('expert', 'shard'), scatter_dimension=0,...  134 us
    reduce_scatter x1, waiting for transfers between devices, body(): lax.psum_scatter(attn_out_grad, ('expert', 'shard'), scatter_dimension=0,...  134 us
    reduce_scatter x1, waiting for transfers between devices, body(): lax.psum_scatter(ctrl_grad, ('expert', 'shard'), scatter_dimension=0, til...  131 us
    dot_general x71, matrix products, product(): return jnp.dot(left_op, right_op, preferred_element_type=jnp.float32)  125 us
  transfers between devices with their start and end apart: 14, of which 8 were waited for; matrix products, arithmetic and copies ran while one was open for 35% of the time, Pallas kernels for 0%

commit v1 on v0

v1 whole, which is shorter than its diff:
```python
import jax
import jax.numpy as jnp
from jax import lax
from jax.experimental import pallas as pl
from jax.experimental.pallas import tpu as pltpu
from jax.sharding import PartitionSpec as P

D = 512
HEAD_DIM = 64
GROUP = 32
ROUTES = 8
BLOCK = 256
CAP = 24
EPSILON = 1e-05
SCALE = 0.125 * 1.4426950408889634
BOTH = ("expert", "shard")

bf16 = jnp.bfloat16
f32 = jnp.float32
VMEM = pltpu.CompilerParams(vmem_limit_bytes=56 * 2**20)


def norm_forward(matrix, scale_vec):
    average = jnp.mean(matrix, axis=1, keepdims=True)
    centered = matrix - average
    inverse = lax.rsqrt(jnp.mean(centered * centered, axis=1, keepdims=True) + EPSILON)
    scaled = centered * inverse
    return (scaled * scale_vec, scaled, inverse)


def norm_input_grad(upstream, scaled, inverse, scale_vec):
    adjusted = upstream * scale_vec
    first_mean = jnp.mean(adjusted, axis=1, keepdims=True)
    second_mean = jnp.mean(adjusted * scaled, axis=1, keepdims=True)
    return inverse * (adjusted - first_mean - scaled * second_mean)


def product(left_op, right_op):
    return jnp.dot(left_op, right_op, preferred_element_type=f32)


def transposed_product(left_op, right_op):
    return lax.dot_general(left_op, right_op, (((0,), (0,)), ((), ())), preferred_element_type=f32)


def against_rows(left_op, right_op):
    return lax.dot_general(left_op, right_op, (((1,), (1,)), ((), ())), preferred_element_type=f32)


def attention_forward_kernel(q_ref, k_ref, v_ref, o_ref, lse_ref):
    length = q_ref.shape[0]
    q_t = q_ref[...].T
    v_t = v_ref[...].T
    zero = jnp.zeros((HEAD_DIM, BLOCK), bf16)
    ones = jnp.ones((16, length), bf16)
    for b in range(length // BLOCK):
        n = (b + 1) * BLOCK
        cols = slice(b * BLOCK, n)
        q_b = q_t[:, cols]
        keys = k_ref[:n, :]
        outs = []
        for h in range(2):
            half = q_b[h * HEAD_DIM : (h + 1) * HEAD_DIM]
            scores = product(keys, jnp.concatenate([half, zero] if h == 0 else [zero, half], 0))
            top = jnp.max(scores, axis=0, keepdims=True)
            weights = jnp.exp2(scores * SCALE - top * SCALE).astype(bf16)
            values = jnp.concatenate([v_t[h * HEAD_DIM : (h + 1) * HEAD_DIM, :n], ones[:, :n]], 0)
            out = product(values, weights)
            total = out[HEAD_DIM : HEAD_DIM + 1]
            outs.append(out[:HEAD_DIM] / total)
            lse_ref[0, h : h + 1, cols] = top * SCALE + jnp.log2(total)
        o_ref[cols, :] = jnp.concatenate(outs, 0).T.astype(bf16)


def attention_backward_kernel(
    q_ref, k_ref, v_ref, g_ref, o_ref, lse_ref, dq_ref, dk_ref, dv_ref, dq_t
):
    length = q_ref.shape[0]
    q = q_ref[...]
    g = g_ref[...]
    q_t = q.T
    g_t = g.T
    k_t = k_ref[...].T
    both = (g.astype(f32) * o_ref[...].astype(f32)).T
    lane = lax.broadcasted_iota(jnp.int32, (1, 2 * HEAD_DIM), 1)
    zero = jnp.zeros((HEAD_DIM, length), bf16)
    heads = []
    for h in range(2):
        rows = slice(h * HEAD_DIM, (h + 1) * HEAD_DIM)
        mine = (lane < HEAD_DIM) if h == 0 else (lane >= HEAD_DIM)
        heads.append(
            (
                rows,
                jnp.concatenate([q_t[rows], zero] if h == 0 else [zero, q_t[rows]], 0),
                jnp.concatenate([g_t[rows], zero] if h == 0 else [zero, g_t[rows]], 0),
                jnp.where(mine, q, 0).astype(bf16),
                jnp.where(mine, g, 0).astype(bf16),
                jnp.sum(both[rows], axis=0, keepdims=True),
                lse_ref[0, h : h + 1, :],
            )
        )
    for j in range(length // BLOCK):
        lo = j * BLOCK
        here = slice(lo, lo + BLOCK)
        keys = k_ref[here, :]
        values = v_ref[here, :]
        key_grad = jnp.zeros((BLOCK, 2 * HEAD_DIM), f32)
        value_grad = jnp.zeros((BLOCK, 2 * HEAD_DIM), f32)
        for rows, q_side, g_side, q_mine, g_mine, delta, lse in heads:
            shares = jnp.exp2(product(keys, q_side[:, lo:]) * SCALE - lse[:, lo:])
            share_grad = product(values, g_side[:, lo:])
            score_grad = (shares * (share_grad - delta[:, lo:])).astype(bf16)
            value_grad = value_grad + product(shares.astype(bf16), g_mine[lo:])
            key_grad = key_grad + product(score_grad, q_mine[lo:])
            query_part = product(k_t[rows, here], score_grad)
            if j == 0:
                dq_t[rows, :] = query_part
            else:
                dq_t[rows, lo:] = dq_t[rows, lo:] + query_part
        dk_ref[here, :] = (key_grad * 0.125).astype(bf16)
        dv_ref[here, :] = value_grad.astype(bf16)
    dq_ref[...] = (dq_t[...] * 0.125).T.astype(bf16)


def pair_columns(length, offset):
    return pl.BlockSpec((length, 2 * HEAD_DIM), lambda pair: (0, pair + offset))


def attention_forward(qkv):
    length = qkv.shape[0]
    pairs = D // (2 * HEAD_DIM)
    stats = pl.BlockSpec((1, 2, length), lambda pair: (pair, 0, 0))
    return pl.pallas_call(
        attention_forward_kernel,
        grid=(pairs,),
        in_specs=[pair_columns(length, i * pairs) for i in range(3)],
        out_specs=[pair_columns(length, 0), stats],
        out_shape=[
            jax.ShapeDtypeStruct((length, D), bf16),
            jax.ShapeDtypeStruct((pairs, 2, length), f32),
        ],
        compiler_params=VMEM,
        cost_estimate=pl.CostEstimate(
            flops=40_000_000_000, bytes_accessed=8 * 2**20, transcendentals=20_000_000
        ),
        name="attention_forward",
    )(qkv, qkv, qkv)


def attention_backward(qkv, grad, attended, lse):
    length = qkv.shape[0]
    pairs = D // (2 * HEAD_DIM)
    stats = pl.BlockSpec((1, 2, length), lambda pair: (pair, 0, 0))
    return pl.pallas_call(
        attention_backward_kernel,
        grid=(pairs,),
        in_specs=[pair_columns(length, i * pairs) for i in range(3)]
        + [pair_columns(length, 0), pair_columns(length, 0), stats],
        out_specs=[pair_columns(length, 0)] * 3,
        out_shape=[jax.ShapeDtypeStruct((length, D), bf16)] * 3,
        scratch_shapes=[pltpu.VMEM((2 * HEAD_DIM, length), f32)],
        compiler_params=VMEM,
        cost_estimate=pl.CostEstimate(
            flops=50_000_000_000, bytes_accessed=16 * 2**20, transcendentals=20_000_000
        ),
        name="attention_backward",
    )(qkv, qkv, qkv, grad, attended, lse)


def gather_rows(block):
    n_shard = lax.axis_size("shard")
    n_expert = lax.axis_size("expert")
    here = lax.axis_index("shard")
    rows, width = block.shape
    held = jnp.zeros((n_shard, rows, width), block.dtype)
    held = lax.dynamic_update_slice(held, block[None], (here, 0, 0))
    for k in range(1, n_shard):
        got = lax.ppermute(block, "shard", [(i, (i + k) % n_shard) for i in range(n_shard)])
        held = lax.dynamic_update_slice(held, got[None], ((here - k) % n_shard, 0, 0))
    held = held.reshape(n_shard * rows, width)
    mine = lax.axis_index("expert")
    bit = n_expert // 2
    steps = 0
    while bit:
        got = lax.ppermute(held, "expert", [(i, i ^ bit) for i in range(n_expert)])
        low = (mine & bit) == 0
        held = jnp.stack([jnp.where(low, held, got), jnp.where(low, got, held)])
        bit //= 2
        steps += 1
    order = tuple(range(steps - 1, -1, -1)) + (steps, steps + 1)
    return held.transpose(order).reshape(n_expert * n_shard * rows, width)


def scatter_sum(partial):
    n_shard = lax.axis_size("shard")
    n_expert = lax.axis_size("expert")
    mine = lax.axis_index("expert")
    width = partial.shape[1]
    steps = n_expert.bit_length() - 1
    held = partial.reshape((2,) * steps + (-1, width))
    for step in range(steps):
        bit = 1 << step
        axis = steps - 1 - step
        low = (mine & bit) == 0
        first = lax.index_in_dim(held, 0, axis, keepdims=False)
        second = lax.index_in_dim(held, 1, axis, keepdims=False)
        away = jnp.where(low, second, first).astype(bf16)
        got = lax.ppermute(away, "expert", [(i, i ^ bit) for i in range(n_expert)])
        held = jnp.where(low, first, second) + got.astype(f32)
    pieces = lax.all_to_all(held.astype(bf16), "shard", split_axis=0, concat_axis=0, tiled=True)
    return jnp.sum(pieces.reshape(n_shard, -1, width).astype(f32), axis=0)


def to_experts(array, copies):
    if copies > 1:
        array = jnp.repeat(array, copies, axis=0)
    return lax.all_to_all(array, "shard", split_axis=0, concat_axis=0, tiled=True)


def from_experts(array, copies):
    back = lax.all_to_all(array, "shard", split_axis=0, concat_axis=0, tiled=True).astype(f32)
    if copies > 1:
        back = back.reshape((-1, copies) + back.shape[1:]).sum(axis=1)
    return back


def exchange(rows, copies):
    n_expert = lax.axis_size("expert")
    n_shard = lax.axis_size("shard")
    groups = None
    if copies > 1:
        groups = [
            [e * n_shard + s for e in range(n_expert) for s in range(p, n_shard, copies)]
            for p in range(copies)
        ]
    return lax.all_to_all(
        rows, BOTH, split_axis=0, concat_axis=0, tiled=True, axis_index_groups=groups
    )


def body(
    tokens,
    ln1_gain,
    ln2_gain,
    w_query,
    w_key,
    w_value,
    w_attn_out,
    w_ctrl,
    w_in,
    b_in,
    w_exp_out,
    routes,
    grad_out,
):
    n_expert = lax.axis_size("expert")
    n_shard = lax.axis_size("shard")
    experts = w_ctrl.shape[1]
    local_count = experts // n_expert
    copies = n_shard // local_count
    length = tokens.shape[0]
    groups = length // GROUP
    hidden = w_in.shape[2]

    small = jnp.concatenate(
        [
            w_query,
            w_key,
            w_value,
            w_attn_out,
            w_ctrl,
            ln1_gain[:, None],
            ln2_gain[:, None],
            jnp.zeros((w_query.shape[0], 128 - experts - 2), f32),
        ],
        axis=1,
    ).astype(bf16)
    whole = gather_rows(small)
    qkv_w = whole[:, : 3 * D]
    attn_out_w = whole[:, 3 * D : 4 * D]
    ctrl_w = whole[:, 4 * D : 4 * D + experts]
    gain_one = whole[:, 4 * D + experts].astype(f32)
    gain_two = whole[:, 4 * D + experts + 1].astype(f32)

    first_block = jnp.concatenate(
        [w_in, jnp.broadcast_to(b_in[:, None, :], (local_count, 16, hidden))], axis=1
    ).astype(bf16)
    whole, first_block, second_block = lax.optimization_barrier(
        (whole, first_block, w_exp_out.astype(bf16))
    )
    first_all = to_experts(first_block, copies)
    second_w = to_experts(second_block, copies)
    first_w = first_all[:, :D, :]
    first_b = first_all[:, D, :]

    inputs = tokens.astype(f32)
    normed_one, scaled_one, inverse_one = norm_forward(inputs, gain_one)
    normed_low = normed_one.astype(bf16)
    qkv = product(normed_low, qkv_w).astype(bf16)
    attended_low, lse = attention_forward(qkv)
    residual = inputs + product(attended_low, attn_out_w)
    normed_two, scaled_two, inverse_two = norm_forward(residual, gain_two)
    normed_mix = normed_two.astype(bf16)
    logits = product(normed_mix, ctrl_w)
    mix_probs = jax.nn.softmax(logits.reshape(groups, GROUP, experts), axis=1)
    selector = (routes[:, :, None] == jnp.arange(experts, dtype=jnp.int32)[None, None, :]).astype(f32)
    chosen = jnp.sum(mix_probs[:, :, None, :] * selector[:, None, :, :], axis=3)
    chosen_low = chosen.astype(bf16)
    members = normed_mix.reshape(groups, GROUP, D)
    members_up = grad_out.reshape(groups, GROUP, D)
    mixed = jnp.einsum("gtk,gtd->gkd", chosen_low, members, preferred_element_type=f32).astype(bf16)
    result_grad = jnp.einsum(
        "gtk,gtd->gkd", chosen_low, members_up, preferred_element_type=f32
    ).astype(bf16)

    named = jnp.sum(selector, axis=1)
    earlier = jnp.tril(jnp.ones((groups, groups), f32), -1)
    before = product(earlier.astype(bf16), named.astype(bf16))
    rank = jnp.sum(selector * before[:, None, :], axis=2).astype(jnp.int32)
    slot_of = (routes * CAP + rank).reshape(-1)
    dispatch = (
        jnp.arange(experts * CAP, dtype=jnp.int32)[:, None] == slot_of[None, :]
    ).astype(bf16)
    rows = jnp.concatenate([mixed.reshape(-1, D), result_grad.reshape(-1, D)], axis=1)
    outgoing = product(dispatch, rows).astype(bf16)
    arrived_all = exchange(outgoing, copies)
    arrived = arrived_all[:, :D]
    arrived_grad = arrived_all[:, D:]

    pre_act = (
        jnp.einsum("rd,sdf->srf", arrived, first_w, preferred_element_type=f32)
        + first_b.astype(f32)[:, None, :]
    )
    sigma = jax.nn.sigmoid(pre_act)
    active = (pre_act * sigma).astype(bf16)
    results = jnp.einsum("srf,sfd->rd", active, second_w, preferred_element_type=f32).astype(bf16)
    hidden_grad = jnp.einsum(
        "rd,sfd->srf", arrived_grad, second_w, preferred_element_type=f32
    ).astype(bf16)
    pre_grad = (hidden_grad.astype(f32) * (sigma * (1.0 + pre_act * (1.0 - sigma)))).astype(bf16)
    mixed_grad_rows = jnp.einsum(
        "srf,sdf->rd", pre_grad, first_w, preferred_element_type=f32
    ).astype(bf16)
    returned = exchange(jnp.concatenate([results, mixed_grad_rows], axis=1), copies)

    first_w_grad = jnp.einsum("rd,srf->sdf", arrived, pre_grad, preferred_element_type=f32)
    first_b_grad = jnp.sum(pre_grad.astype(f32), axis=1)
    second_w_grad = jnp.einsum("srf,rd->sfd", active, arrived_grad, preferred_element_type=f32)
    first_sum = from_experts(
        jnp.concatenate(
            [
                first_w_grad,
                jnp.broadcast_to(first_b_grad[:, None, :], (n_shard, 16, hidden)),
            ],
            axis=1,
        ).astype(bf16),
        copies,
    )
    w_in_grad = first_sum[:, :D, :]
    b_in_grad = first_sum[:, D, :]
    w_exp_out_grad = from_experts(second_w_grad.astype(bf16), copies)

    both_rows = transposed_product(dispatch, returned).astype(bf16)
    gathered_rows = both_rows[:, :D].reshape(groups, ROUTES, D)
    mixed_grad = both_rows[:, D:].reshape(groups, ROUTES, D)
    mixture = jnp.einsum(
        "gtk,gkd->gtd", chosen_low, gathered_rows, preferred_element_type=f32
    ).reshape(length, D)
    output = (residual + mixture).astype(bf16)
    upstream = grad_out.astype(f32)
    chosen_grad = jnp.einsum(
        "gtd,gkd->gtk", members_up, gathered_rows, preferred_element_type=f32
    ) + jnp.einsum("gtd,gkd->gtk", members, mixed_grad, preferred_element_type=f32)
    normed_grad = jnp.einsum(
        "gtk,gkd->gtd", chosen_low, mixed_grad, preferred_element_type=f32
    ).reshape(length, D)
    prob_grad = jnp.sum(chosen_grad[:, :, :, None] * selector[:, None, :, :], axis=2)
    logit_grad = (
        (mix_probs * (prob_grad - jnp.sum(mix_probs * prob_grad, axis=1, keepdims=True)))
        .reshape(length, experts)
        .astype(bf16)
    )
    normed_grad = normed_grad + against_rows(logit_grad, ctrl_w)
    ctrl_grad = transposed_product(normed_mix, logit_grad)
    gain_two_grad = jnp.sum(normed_grad * scaled_two, axis=0)
    residual_grad = upstream + norm_input_grad(normed_grad, scaled_two, inverse_two, gain_two)
    branch_grad = residual_grad.astype(bf16)
    attn_out_grad = transposed_product(attended_low, branch_grad)
    early = scatter_sum(
        jnp.concatenate(
            [
                attn_out_grad,
                ctrl_grad,
                gain_two_grad[:, None],
                jnp.zeros((D, 128 - experts - 1), f32),
            ],
            axis=1,
        )
    )
    wo_grad = early[:, :D]
    wc_grad = early[:, D : D + experts]
    ln2_grad = early[:, D + experts]

    attended_grad = against_rows(branch_grad, attn_out_w).astype(bf16)
    query_grad, key_grad, value_grad = attention_backward(qkv, attended_grad, attended_low, lse)
    late = scatter_sum(
        jnp.concatenate(
            [transposed_product(normed_low, g) for g in (query_grad, key_grad, value_grad)], axis=1
        )
    )
    small_own = small[:, : 3 * D].astype(f32)
    ln1_grad = jnp.sum(late * small_own, axis=1) / small[:, 4 * D + experts].astype(f32)
    normed_one_grad = (
        against_rows(query_grad, qkv_w[:, :D])
        + against_rows(key_grad, qkv_w[:, D : 2 * D])
        + against_rows(value_grad, qkv_w[:, 2 * D :])
    )
    input_grad = (
        residual_grad + norm_input_grad(normed_one_grad, scaled_one, inverse_one, gain_one)
    ).astype(bf16)
    return (
        output,
        input_grad,
        ln1_grad,
        ln2_grad,
        late[:, :D],
        late[:, D : 2 * D],
        late[:, 2 * D :],
        wo_grad,
        wc_grad,
        w_in_grad,
        b_in_grad,
        w_exp_out_grad,
    )


def solution(mesh):
    rows = P(BOTH, None)
    vector = P(BOTH)
    experts = (P("expert", None, "shard"), P("expert", "shard"), P("expert", "shard", None))
    in_specs = (rows, vector, vector) + (rows,) * 5 + experts + (rows, rows)
    out_specs = (rows, rows, vector, vector) + (rows,) * 5 + experts
    return jax.shard_map(body, mesh=mesh, in_specs=in_specs, out_specs=out_specs, check_vma=False)
```

time: 2070 us -> 548 us (0.26)
  waiting for transfers between devices: 746 us -> 146 us
  blocking collectives: 538 us -> 54.7 us
  matrix products: 531 us -> 86.9 us
  Pallas kernels: 0 us -> 104 us
  local copies, waits for them, and re-layouts: 110 us -> 53.7 us
  other arithmetic: 93.5 us -> 49.9 us
  starting transfers between devices: 20.1 us -> 44.3 us
    reduce_scatter x8 -> x0, waiting for transfers between devices: 741 us -> none  [the longest x1 134 us: body(): lax.psum_scatter(value_w_grad, ('expert', 'shard'), scatter_dimension=0,...]
    all_gather x6 -> x0, blocking collectives: 442 us -> none  [the longest x1 98.5 us: body(): lax.all_gather(w_key.astype(jnp.bfloat16), ('expert', 'shard'), axis=0, t...]
    dot_general x101 -> x5, matrix products: 188 us -> 24.1 us  [against_rows(): lax.dot_general(left_op, right_op, (((1,), (1,)), ((), ())), preferred_el...]
    dot_general x78 -> x14, matrix products: 192 us -> 46.3 us  [the longest x5 11.4 us: product(): return jnp.dot(left_op, right_op, preferred_element_type=f32)]
    dot_general x71 -> x5, matrix products: 144 us -> 9.45 us  [transposed_product(): lax.dot_general(left_op, right_op, (((0,), (0,)), ((), ())), preferred_el...]
    all_to_all x4 -> x7, waiting for transfers between devices: 5.35 us -> 124 us  [the longest x2 46.2 us: exchange(): lax.all_to_all(rows, BOTH, split_axis=0, concat_axis=0, tiled=True, axis_...]
    pallas_call x0 -> x2, Pallas kernels: none -> 104 us  [the longest x1 53.3 us: attention_backward(): pl.pallas_call(attention_backward_kernel, grid=(pairs,), in_specs=[pair_c...]
    unnamed x2 -> x0, blocking collectives: 95.7 us -> none
  transfers between devices with their start and end apart: 14 -> 20, of which waited for: 8 -> 11; matrix products, arithmetic and copies ran while one was open for 35% -> 25% of each run, Pallas kernels for 0% -> 10%
where the time goes in v1:
time: 548 us; the launch traced here: 542 us
  waiting for transfers between devices  146 us (27%)
  Pallas kernels  104 us (19%)
  matrix products  86.9 us (16%)
  blocking collectives  54.7 us (10%)
  local copies, waits for them, and re-layouts  53.7 us (10%)
  other arithmetic  49.9 us (9%)
  starting transfers between devices  44.3 us (8%)
    all_to_all x1, blocking collectives, to_experts(): lax.all_to_all(array, 'shard', split_axis=0, concat_axis=0, tiled=True)  54.7 us
    pallas_call x1, Pallas kernels, attention_backward(): pl.pallas_call(attention_backward_kernel, grid=(pairs,), in_specs=[pair_c...  53.3 us
    pallas_call x1, Pallas kernels, attention_forward(): pl.pallas_call(attention_forward_kernel, grid=(pairs,), in_specs=[pair_co...  50.8 us
    all_to_all x2, waiting for transfers between devices, exchange(): lax.all_to_all(rows, BOTH, split_axis=0, concat_axis=0, tiled=True, axis_...  46.2 us
    all_to_all x1, waiting for transfers between devices, to_experts(): lax.all_to_all(array, 'shard', split_axis=0, concat_axis=0, tiled=True)  37.9 us
    all_to_all x2, waiting for transfers between devices, from_experts(): lax.all_to_all(array, 'shard', split_axis=0, concat_axis=0, tiled=True)  30.5 us
    dot_general x5, matrix products, against_rows(): lax.dot_general(left_op, right_op, (((1,), (1,)), ((), ())), preferred_el...  24.1 us
    unnamed x120, local copies, waits for them, and re-layouts  21.9 us
  transfers between devices with their start and end apart: 20, of which 11 were waited for; matrix products, arithmetic and copies ran while one was open for 25% of the time, Pallas kernels for 10%

profile of v1, /device:TPU:0, one launch (start us, length us, event | category | flops | bytes accessed | tf_op | source)
XLA Modules:
  0.0 541.6 jit_solution(5682400094687532770)
XLA Ops:
  6.0 6.0 %collective-permute-start.6 = (bf16[16,2176]{1,0:T(8,128)(2,1)S(1)}, bf16[16,2176]{1,0:T(8,128)(2,1)S(1)}, u32[]{:S(2)}, u32[]{:S(2)}) collective-permute-start(bf16[16,2176]{1,0:T(8,128)(2,1)S(1)} %concatenate.66), channel_id=1, source_target_pairs={{0,7},{1,0},{2,1},{3,2},{4,3},{5,4},{6,5},{7,6},{8,15},{9,8},{10,9... | collective-permute-start | bytes 208904 | tf_op jit(solution)/shard_map/ppermute | solution.py:178
  12.5 3.0 collective-permute-start.3
  15.5 1.5 collective-permute-start
  22.5 6.1 %collective-permute-done.1 = bf16[16,2176]{1,0:T(8,128)(2,1)S(1)} collective-permute-done((bf16[16,2176]{1,0:T(8,128)(2,1)S(1)}, bf16[16,2176]{1,0:T(8,128)(2,1)S(1)}, u32[]{:S(2)}, u32[]{:S(2)}) %collective-permute-start.1) | collective-permute-done | bytes 69664 | tf_op jit(solution)/shard_map/ppermute | solution.py:178
  28.6 6.1 %collective-permute-done.2 = bf16[16,2176]{1,0:T(8,128)(2,1)S(1)} collective-permute-done((bf16[16,2176]{1,0:T(8,128)(2,1)S(1)}, bf16[16,2176]{1,0:T(8,128)(2,1)S(1)}, u32[]{:S(2)}, u32[]{:S(2)}) %collective-permute-start.2) | collective-permute-done | bytes 69664 | tf_op jit(solution)/shard_map/ppermute | solution.py:178
  34.8 1.6 collective-permute-start.7
  37.4 8.0 %collective-permute-done.7 = bf16[128,2176]{1,0:T(8,128)(2,1)S(1)} collective-permute-done((bf16[128,2176]{1,0:T(8,128)(2,1)S(1)}, bf16[128,2176]{1,0:T(8,128)(2,1)S(1)}, u32[]{:S(2)}, u32[]{:S(2)}) %collective-permute-start.7) | collective-permute-done | bytes 557088 | tf_op jit(solution)/shard_map/ppermute | solution.py:185
  47.2 1.3 collective-permute-done.8
  50.3 1.3 copy-done.25
  51.6 5.4 convolution_convert_fusion.q_ref.k_ref.v_ref
  57.0 50.8 %attention_forward.1 = (bf16[2048,512]{1,0:T(8,128)(2,1)}, f32[4,2,2048]{2,1,0:T(2,128)}) custom-call(bf16[2048,1536]{1,0:T(8,128)(2,1)} %convolution_convert_fusion.q_ref.k_ref.v_ref, bf16[2048,1536]{1,0:T(8,128)(2,1)} %convolution_convert_fusion.q_ref.k_ref.v_ref, bf16[2048,1536]{1,0:T(8,128)(2,1)} %convolution_convert_fusion.q_ref.k_ref.v_ref), custom_call_target="tpu_custom_call" | custom-call | flops 40000000000 | bytes 8388608 | tf_op jit(solution)/shard_map/attention_forward/pallas_call | solution.py:133
  107.9 3.0 fusion.75
  118.8 2.0 fusion.30
  121.2 2.1 convolution_convert_fusion.3
  123.3 3.5 all-to-all-start.1
  126.9 3.7 convert.68
  130.6 4.6 copy.127
  135.2 3.1 pad_maximum_fusion.3
  138.3 27.4 %all-to-all-done.1 = bf16[32,24,1024]{2,1,0:T(8,128)(2,1)} async-done(((bf16[32,24,1024]{2,1,0:T(8,128)(2,1)}), bf16[32,24,1024]{2,1,0:T(8,128)(2,1)}, u32[]{:S(2)}, u32[]{:S(2)}) %all-to-all-start.1) | async-done | bytes 1572896 | tf_op jit(solution)/shard_map/all_to_all | solution.py:236
  165.7 54.7 %all_to_all.62 = bf16[8,528,256]{2,1,0:T(8,128)(2,1)} all-to-all(bf16[8,528,256]{2,1,0:T(8,128)(2,1)} %pad_maximum_fusion.3), channel_id=1, replica_groups=mesh['expert'=4,'shard'=8] {'shard'}, dimensions={0} | all-to-all | bytes 4325376 | tf_op jit(solution)/shard_map/all_to_all | solution.py:217
  220.4 4.8 all-to-all-start.2
  225.9 8.6 %fusion.4 = (bf16[8,768,256]{1,2,0:T(8,128)(2,1)}, f32[8,256,768]{2,1,0:T(8,128)}) fusion(f32[8,256]{1,0:T(8,128)S(1)} %fusion.68, bf16[768,1024]{1,0:T(8,128)(2,1)} %bitcast.30, bf16[8,528,256]{2,1,0:T(8,128)(2,1)} %all_to_all.62), kind=kOutput, calls=%fused_computation.9 | convolution fusion | flops 1620049920 | bytes 12328960 | tf_op jit(solution)/shard_map/rd,sdf->srf/dot_general | solution.py:331
  234.6 37.9 %all-to-all-done.2 = bf16[8,256,512]{1,2,0:T(8,128)(2,1)} async-done(((bf16[8,256,512]{1,2,0:T(8,128)(2,1)}), bf16[8,256,512]{1,2,0:T(8,128)(2,1)}, u32[]{:S(2)}, u32[]{:S(2)}) %all-to-all-start.2) | async-done | bytes 2097184 | tf_op jit(solution)/shard_map/all_to_all | solution.py:217
  272.4 7.8 %fusion.76 = (bf16[8,256]{1,0:T(8,128)(2,1)}, bf16[8,768,256]{1,2,0:T(8,128)(2,1)S(1)}) fusion(f32[8,256,768]{2,1,0:T(8,128)} %get-tuple-element.99, f32[8,256]{1,0:T(8,128)S(1)} %fusion.68, bf16[8,256,512]{1,2,0:T(8,128)(2,1)} %all-to-all-done.2, bf16[768,1024]{1,0:T(8,128)(2,1)} %bitcast.30), kind=kOutput, calls=%fused_computation.168 | convolution fusion | flops 1631057920 | bytes 12333056 | tf_op jit(solution)/shard_map/rd,sfd->srf/dot_general | solution.py:337
  280.2 4.6 bitcast_convert_fusion.1
  284.8 1.8 bitcast_convert_fusion
  287.9 2.6 copy.136
  290.5 3.9 all-to-all-start.3
  298.9 3.9 convert_bitcast_fusion
  303.1 1.8 pad_maximum_fusion.1
  304.9 4.3 copy.155
  309.2 5.2 convolution_convert_fusion.2
  314.4 18.8 %all-to-all-done.3 = bf16[32,24,1024]{2,1,0:T(8,128)(2,1)} async-done(((bf16[32,24,1024]{2,1,0:T(8,128)(2,1)}), bf16[32,24,1024]{2,1,0:T(8,128)(2,1)}, u32[]{:S(2)}, u32[]{:S(2)}) %all-to-all-start.3) | async-done | bytes 1572896 | tf_op jit(solution)/shard_map/all_to_all | solution.py:236
  333.2 4.4 all-to-all-start.7
  337.6 2.6 fusion.26
  340.9 2.8 fusion.53
  343.6 2.8 fusion.52
  348.7 1.4 copy.142
  353.5 4.8 multiply_reduce_fusion
  360.1 3.3 multiply_add_fusion
  363.4 1.3 fusion.34
  365.4 3.7 convolution_convert_fusion.1.g_ref
  371.3 53.3 %attention_backward.1 = (bf16[2048,512]{1,0:T(8,128)(2,1)}, bf16[2048,512]{1,0:T(8,128)(2,1)}, bf16[2048,512]{1,0:T(8,128)(2,1)}) custom-call(bf16[2048,1536]{1,0:T(8,128)(2,1)} %convolution_convert_fusion.q_ref.k_ref.v_ref, bf16[2048,1536]{1,0:T(8,128)(2,1)} %convolution_convert_fusion.q_ref.k_ref.v_ref, ...), custom_call_target="tpu_custom_call" | custom-call | flops 49999998976 | bytes 16777216 | tf_op jit(solution)/shard_map/attention_backward/pallas_call | solution.py:154
  424.6 3.0 fusion.77
  427.6 1.3 fusion.78
  429.2 1.3 fusion.79
  430.8 3.3 reshape.302
  434.1 6.5 %fusion.73 = (f32[2,1,128,1536]{2,1,0,3:T(1,128)S(1)}, f32[2,1,128,1536]{2,1,0,3:T(1,128)}) fusion(f32[2,2,128,1536]{2,1,0,3:T(2,128)} %reshape.302), kind=kLoop, calls=%fused_computation.165 | loop fusion | bytes 6291456 | tf_op jit(solution)/shard_map/slice | solution.py:205
  440.6 1.9 copy.169
  442.6 3.8 copy.170
  448.9 4.4 fusion.44
  453.2 4.4 fusion.46
  457.7 6.3 %all-to-all-start.6 = ((bf16[8,528,256]{2,1,0:T(8,128)(2,1)}), bf16[8,528,256]{2,1,0:T(8,128)(2,1)}, u32[]{:S(2)}, u32[]{:S(2)}) async-start(bf16[8,528,256]{2,1,0:T(8,128)(2,1)} %copy.155), calls=%async_computation.6 | async-start | bytes 4325376 | tf_op jit(solution)/shard_map/all_to_all | solution.py:221
  464.0 6.8 %fusion.72 = (f32[2048]{0:T(1024)S(1)}, f32[2048]{0:T(1024)S(1)}, f32[2048,512]{1,0:T(8,128)S(1)}) fusion(f32[2048]{0:T(1024)S(1)} %copy-done.42, f32[2048]{0:T(1024)S(1)} %copy-done.32, bf16[2048,512]{1,0:T(8,128)(2,1)S(1)} %copy-done.3, f32[512]{0:T(512)S(1)} %copy-done.49, bf16[2048,512]{1,0:T(8,128)(2,1)} %get-tuple-element.25, ...), kind=kOutput, calls=%fused_computation.164 | convolution fusion | flops 1083174912 | bytes 17336320 | tf_op jit(solution)/shard_map/dot_general | solution.py:47
  472.2 1.8 bitcast_add_fusion.2
  475.9 2.8 fusion.17
  479.5 4.3 convert_element_type.238
  483.8 30.5 %all-to-all-done.6 = bf16[8,528,256]{2,1,0:T(8,128)(2,1)} async-done(((bf16[8,528,256]{2,1,0:T(8,128)(2,1)}), bf16[8,528,256]{2,1,0:T(8,128)(2,1)}, u32[]{:S(2)}, u32[]{:S(2)}) %all-to-all-start.6) | async-done | bytes 2162720 | tf_op jit(solution)/shard_map/all_to_all | solution.py:221
  514.3 3.6 all-to-all-start.5
  518.8 6.8 %all-to-all-done.5 = bf16[8,16,640]{2,1,0:T(8,128)(2,1)S(1)} async-done(((bf16[8,16,640]{2,1,0:T(8,128)(2,1)}), bf16[8,16,640]{2,1,0:T(8,128)(2,1)S(1)}, u32[]{:S(2)}, u32[]{:S(2)}) %all-to-all-start.5) | async-done | bytes 163872 | tf_op jit(solution)/shard_map/all_to_all | solution.py:210
  525.6 3.5 all-to-all-start.4
  529.1 2.3 copy_convert_fusion
  531.7 3.3 copy.157
  537.5 2.5 all-to-all-done.4
  (238 shorter events, 53.9 us)
Async XLA Ops:
  0.6 36.0 %copy-start.45 = (s32[64,8]{0,1:T(8,128)S(1)}, s32[64,8]{0,1:T(8,128)}, u32[]{:S(2)}) copy-start(s32[64,8]{0,1:T(8,128)} %param.24) | copy-start | bytes 6148
  3.6 18.1 %copy-start.35 = (bf16[16,512]{1,0:T(8,128)(2,1)}, bf16[16,512]{1,0:T(8,128)(2,1)S(1)}, u32[]{:S(2)}) copy-start(bf16[16,512]{1,0:T(8,128)(2,1)S(1)} %convert.61) | copy-start | bytes 49156
  4.4 17.3 %copy-start.37 = (bf16[16,512]{1,0:T(8,128)(2,1)}, bf16[16,512]{1,0:T(8,128)(2,1)S(1)}, u32[]{:S(2)}) copy-start(bf16[16,512]{1,0:T(8,128)(2,1)S(1)} %convert.62) | copy-start | bytes 49156
  5.2 16.6 %copy-start.39 = (bf16[16,512]{1,0:T(8,128)(2,1)}, bf16[16,512]{1,0:T(8,128)(2,1)S(1)}, u32[]{:S(2)}) copy-start(bf16[16,512]{1,0:T(8,128)(2,1)S(1)} %convert.63) | copy-start | bytes 49156
  6.0 28.8 %collective-permute-start.6 = (bf16[16,2176]{1,0:T(8,128)(2,1)S(1)}, bf16[16,2176]{1,0:T(8,128)(2,1)S(1)}, u32[]{:S(2)}, u32[]{:S(2)}) collective-permute-start(bf16[16,2176]{1,0:T(8,128)(2,1)S(1)} %concatenate.66), channel_id=1, source_target_pairs={{0,7},{1,0},{2,1},{3,2},{4,3},{5,4},{6,5},{7,6},{8,15},{9,8},{10,9... | collective-permute-start | bytes 208904 | tf_op jit(solution)/shard_map/ppermute | solution.py:178
  12.1 22.7 %collective-permute-start.5 = (bf16[16,2176]{1,0:T(8,128)(2,1)S(1)}, bf16[16,2176]{1,0:T(8,128)(2,1)S(1)}, u32[]{:S(2)}, u32[]{:S(2)}) collective-permute-start(bf16[16,2176]{1,0:T(8,128)(2,1)S(1)} %concatenate.66), channel_id=1, source_target_pairs={{0,6},{1,7},{2,0},{3,1},{4,2},{5,3},{6,4},{7,5},{8,14},{9,15},{10,... | collective-permute-start | bytes 208904 | tf_op jit(solution)/shard_map/ppermute | solution.py:178
  12.5 22.3 %collective-permute-start.4 = (bf16[16,2176]{1,0:T(8,128)(2,1)S(1)}, bf16[16,2176]{1,0:T(8,128)(2,1)S(1)}, u32[]{:S(2)}, u32[]{:S(2)}) collective-permute-start(bf16[16,2176]{1,0:T(8,128)(2,1)S(1)} %concatenate.66), channel_id=1, source_target_pairs={{0,5},{1,6},{2,7},{3,0},{4,1},{5,2},{6,3},{7,4},{8,13},{9,14},{10,... | collective-permute-start | bytes 208904 | tf_op jit(solution)/shard_map/ppermute | solution.py:178
  12.5 22.2 %collective-permute-start.3 = (bf16[16,2176]{1,0:T(8,128)(2,1)S(1)}, bf16[16,2176]{1,0:T(8,128)(2,1)S(1)}, u32[]{:S(2)}, u32[]{:S(2)}) collective-permute-start(bf16[16,2176]{1,0:T(8,128)(2,1)S(1)} %concatenate.66), channel_id=1, source_target_pairs={{0,4},{1,5},{2,6},{3,7},{4,0},{5,1},{6,2},{7,3},{8,12},{9,13},{10,... | collective-permute-start | bytes 208904 | tf_op jit(solution)/shard_map/ppermute | solution.py:178
  15.5 7.0 %collective-permute-start = (bf16[16,2176]{1,0:T(8,128)(2,1)S(1)}, bf16[16,2176]{1,0:T(8,128)(2,1)S(1)}, u32[]{:S(2)}, u32[]{:S(2)}) collective-permute-start(bf16[16,2176]{1,0:T(8,128)(2,1)S(1)} %concatenate.66), channel_id=1, source_target_pairs={{0,1},{1,2},{2,3},{3,4},{4,5},{5,6},{6,7},{7,0},{8,9},{9,10},{10,1... | collective-permute-start | bytes 208904 | tf_op jit(solution)/shard_map/ppermute | solution.py:178
  22.5 6.1 %collective-permute-start.1 = (bf16[16,2176]{1,0:T(8,128)(2,1)S(1)}, bf16[16,2176]{1,0:T(8,128)(2,1)S(1)}, u32[]{:S(2)}, u32[]{:S(2)}) collective-permute-start(bf16[16,2176]{1,0:T(8,128)(2,1)S(1)} %concatenate.66), channel_id=1, source_target_pairs={{0,2},{1,3},{2,4},{3,5},{4,6},{5,7},{6,0},{7,1},{8,10},{9,11},{10,... | collective-permute-start | bytes 208904 | tf_op jit(solution)/shard_map/ppermute | solution.py:178
  28.6 6.1 %collective-permute-start.2 = (bf16[16,2176]{1,0:T(8,128)(2,1)S(1)}, bf16[16,2176]{1,0:T(8,128)(2,1)S(1)}, u32[]{:S(2)}, u32[]{:S(2)}) collective-permute-start(bf16[16,2176]{1,0:T(8,128)(2,1)S(1)} %concatenate.66), channel_id=1, source_target_pairs={{0,3},{1,4},{2,5},{3,6},{4,7},{5,0},{6,1},{7,2},{8,11},{9,12},{10,... | collective-permute-start | bytes 208904 | tf_op jit(solution)/shard_map/ppermute | solution.py:178
  34.8 10.5 %collective-permute-start.7 = (bf16[128,2176]{1,0:T(8,128)(2,1)S(1)}, bf16[128,2176]{1,0:T(8,128)(2,1)S(1)}, u32[]{:S(2)}, u32[]{:S(2)}) collective-permute-start(bf16[128,2176]{1,0:T(8,128)(2,1)S(1)} %bitcast.223), channel_id=1, source_target_pairs={{0,16},{8,24},{16,0},{24,8},{1,17},{9,25},{17,1},{25,9},{2,18},{10... | collective-permute-start | bytes 1671176 | tf_op jit(solution)/shard_map/ppermute | solution.py:185
  37.4 8.4 %copy-start.2 = (bf16[2048,512]{1,0:T(8,128)(2,1)S(1)}, bf16[2048,512]{1,0:T(8,128)(2,1)}, u32[]{:S(2)}) copy-start(bf16[2048,512]{1,0:T(8,128)(2,1)} %param.13) | copy-start | bytes 6291460
  45.7 2.8 collective-permute-start.8
  46.1 3.1 copy-start.31
  47.2 70.6 %copy-start.27 = (f32[64,8,32]{0,2,1:T(8,128)}, f32[64,8,32]{0,2,1:T(8,128)S(1)}, u32[]{:S(2)}) copy-start(f32[64,8,32]{0,2,1:T(8,128)S(1)} %fusion.58) | copy-start | bytes 196612
  49.0 63.5 %copy-start.14 = (bf16[2,2,128,2176]{3,2,0,1:T(8,128)(2,1)}, bf16[2,2,128,2176]{3,2,0,1:T(8,128)(2,1)S(1)}, u32[]{:S(2)}) copy-start(bf16[2,2,128,2176]{3,2,0,1:T(8,128)(2,1)S(1)} %pad_maximum_fusion.2) | copy-start | bytes 6684676
  49.2 7.8 %copy-start.48 = (f32[512]{0:T(512)}, f32[512]{0:T(512)S(1)}, u32[]{:S(2)}) copy-start(f32[512]{0:T(512)S(1)} %get-tuple-element.80) | copy-start | bytes 6148
  49.3 62.5 %copy-start.46 = (f32[512]{0:T(512)}, f32[512]{0:T(512)S(1)}, u32[]{:S(2)}) copy-start(f32[512]{0:T(512)S(1)} %get-tuple-element.79) | copy-start | bytes 6148
  116.6 4.1 copy-start.29
  118.8 2.4 copy-start.53
  123.3 3.6 copy-start.51
  123.3 42.4 %all-to-all-start.1 = ((bf16[32,24,1024]{2,1,0:T(8,128)(2,1)}), bf16[32,24,1024]{2,1,0:T(8,128)(2,1)}, u32[]{:S(2)}, u32[]{:S(2)}) async-start(bf16[32,24,1024]{2,1,0:T(8,128)(2,1)} %bitcast.224), calls=%async_computation.1 | async-start | bytes 3145728 | tf_op jit(solution)/shard_map/all_to_all | solution.py:236
  220.4 52.1 %all-to-all-start.2 = ((bf16[8,256,512]{1,2,0:T(8,128)(2,1)}), bf16[8,256,512]{1,2,0:T(8,128)(2,1)}, u32[]{:S(2)}, u32[]{:S(2)}) async-start(bf16[8,256,512]{1,2,0:T(8,128)(2,1)} %copy.127), calls=%async_computation.2 | async-start | bytes 4194304 | tf_op jit(solution)/shard_map/all_to_all | solution.py:217
  272.4 7.8 %copy-start.56 = (bf16[8,768,256]{1,2,0:T(8,128)(2,1)S(1)}, bf16[8,768,256]{1,2,0:T(8,128)(2,1)}, u32[]{:S(2)}) copy-start(bf16[8,768,256]{1,2,0:T(8,128)(2,1)} %get-tuple-element.98) | copy-start | bytes 9437188
  280.2 4.6 copy-start.57
  280.2 4.6 copy-start.23
  290.5 42.7 %all-to-all-start.3 = ((bf16[32,24,1024]{2,1,0:T(8,128)(2,1)}), bf16[32,24,1024]{2,1,0:T(8,128)(2,1)}, u32[]{:S(2)}, u32[]{:S(2)}) async-start(bf16[32,24,1024]{2,1,0:T(8,128)(2,1)} %bitcast.221), calls=%async_computation.3 | async-start | bytes 3145728 | tf_op jit(solution)/shard_map/all_to_all | solution.py:236
  298.9 3.9 copy-start.52
  314.4 23.2 %copy-start.54 = (s32[512]{0:T(512)S(1)}, s32[512]{0:T(512)}, u32[]{:S(2)}) copy-start(s32[512]{0:T(512)} %eq.56) | copy-start | bytes 6148
  333.2 124.4 %all-to-all-start.7 = ((bf16[8,256,512]{2,1,0:T(8,128)(2,1)}), bf16[8,256,512]{2,1,0:T(8,128)(2,1)}, u32[]{:S(2)}, u32[]{:S(2)}) async-start(bf16[8,256,512]{2,1,0:T(8,128)(2,1)} %convolution_convert_fusion.2), calls=%async_computation.7 | async-start | bytes 4194304 | tf_op jit(solution)/shard_map/all_to_all | solution.py:221
  337.6 2.6 copy-start.6
  350.1 3.3 copy-start.34
  350.1 3.3 copy-start.44
  353.5 4.9 copy-start.1
  353.5 5.4 copy-start.7
  353.5 6.6 %copy-start.8 = (f32[64,32,512]{2,1,0:T(8,128)S(1)}, f32[64,32,512]{2,1,0:T(8,128)}, u32[]{:S(2)}) copy-start(f32[64,32,512]{2,1,0:T(8,128)} %fusion.52) | copy-start | bytes 12582916
  360.1 3.3 copy-start.9
  365.4 3.8 copy-start.50
  371.3 99.6 %collective-permute-start.11 = (bf16[2,128,640]{2,1,0:T(8,128)(2,1)}, bf16[2,128,640]{2,1,0:T(8,128)(2,1)S(1)}, u32[]{:S(2)}, u32[]{:S(2)}) collective-permute-start(bf16[2,128,640]{2,1,0:T(8,128)(2,1)} %fusion.55), channel_id=1, source_target_pairs={{0,8},{8,0},{16,24},{24,16},{1,9},{9,1},{17,25},{25,17},{2,10},{10... | collective-permute-start | bytes 983048 | tf_op jit(solution)/shard_map/ppermute | solution.py:208
  371.3 53.3 %copy-start.26 = (bf16[2048,512]{1,0:T(8,128)(2,1)S(1)}, bf16[2048,512]{1,0:T(8,128)(2,1)}, u32[]{:S(2)}) copy-start(bf16[2048,512]{1,0:T(8,128)(2,1)} %copy-done.25) | copy-start | bytes 6291460
  424.6 3.0 copy-start.21
  442.6 4.9 copy-start.10
  446.4 6.8 %copy-start.12 = (f32[2,1,128,1536]{3,2,0,1:T(8,128)}, f32[2,1,128,1536]{3,2,0,1:T(8,128)S(1)}, u32[]{:S(2)}) copy-start(f32[2,1,128,1536]{3,2,0,1:T(8,128)S(1)} %copy.170) | copy-start | bytes 4718596
  446.4 2.4 copy-start.22
  447.5 5.7 %copy-start.20 = (bf16[2048,512]{1,0:T(8,128)(2,1)S(1)}, bf16[2048,512]{1,0:T(8,128)(2,1)}, u32[]{:S(2)}) copy-start(bf16[2048,512]{1,0:T(8,128)(2,1)} %get-tuple-element.23) | copy-start | bytes 6291460
  447.5 24.1 %collective-permute-start.9 = (bf16[2,128,1536]{2,1,0:T(8,128)(2,1)}, bf16[2,128,1536]{2,1,0:T(8,128)(2,1)}, u32[]{:S(2)}, u32[]{:S(2)}) collective-permute-start(bf16[2,128,1536]{2,1,0:T(8,128)(2,1)} %fusion.37), channel_id=1, source_target_pairs={{0,8},{8,0},{16,24},{24,16},{1,9},{9,1},{17,25},{25,17},{2,10},{10... | collective-permute-start | bytes 2359304 | tf_op jit(solution)/shard_map/ppermute | solution.py:208
  457.6 6.3 %copy-start.3 = (bf16[2048,512]{1,0:T(8,128)(2,1)S(1)}, bf16[2048,512]{1,0:T(8,128)(2,1)}, u32[]{:S(2)}) copy-start(bf16[2048,512]{1,0:T(8,128)(2,1)} %param.13) | copy-start | bytes 6291460
  457.6 6.3 %copy-start.32 = (f32[2048]{0:T(1024)S(1)}, f32[2048]{0:T(1024)}, u32[]{:S(2)}) copy-start(f32[2048]{0:T(1024)} %copy-done.31) | copy-start | bytes 24580
  457.7 6.3 %copy-start.42 = (f32[2048]{0:T(1024)S(1)}, f32[2048]{0:T(1024)}, u32[]{:S(2)}) copy-start(f32[2048]{0:T(1024)} %copy-done.41) | copy-start | bytes 24580
  457.7 6.3 %copy-start.49 = (f32[512]{0:T(512)S(1)}, f32[512]{0:T(512)}, u32[]{:S(2)}) copy-start(f32[512]{0:T(512)} %copy-done.48) | copy-start | bytes 6148
  457.7 56.6 %all-to-all-start.6 = ((bf16[8,528,256]{2,1,0:T(8,128)(2,1)}), bf16[8,528,256]{2,1,0:T(8,128)(2,1)}, u32[]{:S(2)}, u32[]{:S(2)}) async-start(bf16[8,528,256]{2,1,0:T(8,128)(2,1)} %copy.155), calls=%async_computation.6 | async-start | bytes 4325376 | tf_op jit(solution)/shard_map/all_to_all | solution.py:221
  464.0 6.9 %copy-start.19 = (f32[2,2,128,640]{3,2,1,0:T(8,128)S(1)}, f32[2,2,128,640]{3,2,1,0:T(8,128)}, u32[]{:S(2)}) copy-start(f32[2,2,128,640]{3,2,1,0:T(8,128)} %copy-done.18) | copy-start | bytes 3932164
  464.0 7.7 %copy-start.13 = (f32[2,1,128,1536]{3,2,0,1:T(8,128)S(1)}, f32[2,1,128,1536]{3,2,0,1:T(8,128)}, u32[]{:S(2)}) copy-start(f32[2,1,128,1536]{3,2,0,1:T(8,128)} %copy-done.12) | copy-start | bytes 4718596
  471.0 4.9 copy-start.5
  471.0 7.7 %collective-permute-start.12 = (bf16[128,640]{1,0:T(8,128)(2,1)S(1)}, bf16[128,640]{1,0:T(8,128)(2,1)S(1)}, u32[]{:S(2)}, u32[]{:S(2)}) collective-permute-start(bf16[128,640]{1,0:T(8,128)(2,1)S(1)} %fusion.57), channel_id=1, source_target_pairs={{0,16},{8,24},{16,0},{24,8},{1,17},{9,25},{17,1},{25,9},{2,18},{10... | collective-permute-start | bytes 491528 | tf_op jit(solution)/shard_map/ppermute | solution.py:208
  475.2 42.7 %collective-permute-start.10 = (bf16[128,1536]{1,0:T(8,128)(2,1)S(1)}, bf16[128,1536]{1,0:T(8,128)(2,1)S(1)}, u32[]{:S(2)}, u32[]{:S(2)}) collective-permute-start(bf16[128,1536]{1,0:T(8,128)(2,1)S(1)} %fusion.54), channel_id=1, source_target_pairs={{0,16},{8,24},{16,0},{24,8},{1,17},{9,25},{17,1},{25,9},{2,18},{10... | collective-permute-start | bytes 1179656 | tf_op jit(solution)/shard_map/ppermute | solution.py:208
  479.5 38.4 %copy-start.16 = (f32[2,128,1536]{2,1,0:T(8,128)S(1)}, f32[2,128,1536]{2,1,0:T(8,128)}, u32[]{:S(2)}) copy-start(f32[2,128,1536]{2,1,0:T(8,128)} %copy-done.15) | copy-start | bytes 4718596
  514.3 11.3 %all-to-all-start.5 = ((bf16[8,16,640]{2,1,0:T(8,128)(2,1)}), bf16[8,16,640]{2,1,0:T(8,128)(2,1)S(1)}, u32[]{:S(2)}, u32[]{:S(2)}) async-start(bf16[8,16,640]{2,1,0:T(8,128)(2,1)} %bitcast.60), calls=%async_computation.5 | async-start | bytes 327680 | tf_op jit(solution)/shard_map/all_to_all | solution.py:210
  525.6 14.4 %all-to-all-start.4 = ((bf16[8,16,1536]{2,1,0:T(8,128)(2,1)}), bf16[8,16,1536]{2,1,0:T(8,128)(2,1)S(1)}, u32[]{:S(2)}, u32[]{:S(2)}) async-start(bf16[8,16,1536]{2,1,0:T(8,128)(2,1)} %bitcast.49), calls=%async_computation.4 | async-start | bytes 786432 | tf_op jit(solution)/shard_map/all_to_all | solution.py:210
  531.6 8.4 %copy-start.36 = (bf16[16,512]{1,0:T(8,128)(2,1)S(1)}, bf16[16,512]{1,0:T(8,128)(2,1)}, u32[]{:S(2)}) copy-start(bf16[16,512]{1,0:T(8,128)(2,1)} %copy-done.35) | copy-start | bytes 49156
  531.7 8.4 %copy-start.38 = (bf16[16,512]{1,0:T(8,128)(2,1)S(1)}, bf16[16,512]{1,0:T(8,128)(2,1)}, u32[]{:S(2)}) copy-start(bf16[16,512]{1,0:T(8,128)(2,1)} %copy-done.37) | copy-start | bytes 49156
  531.7 8.4 %copy-start.40 = (bf16[16,512]{1,0:T(8,128)(2,1)S(1)}, bf16[16,512]{1,0:T(8,128)(2,1)}, u32[]{:S(2)}) copy-start(bf16[16,512]{1,0:T(8,128)(2,1)} %copy-done.39) | copy-start | bytes 49156
  531.7 9.2 %copy-start.55 = (f32[16]{0:T(128)S(1)}, f32[16]{0:T(128)}, u32[]{:S(2)}) copy-start(f32[16]{0:T(128)} %param.14) | copy-start | bytes 196
  (14 other events, 21.5 us)
